TPU v7x, 128 devices: a whole 4x4x4 slice. The times are simulated.
128 devices in a mesh: dp: 8 (over y, core), mp: 16 (over z, x).
Axes of the slice: x: 4, y: 4, z: 4, core: 2. Of those that a mesh axis runs over, the one named last changes fastest.
Arguments:
- momentum: bfloat16 [8, 5120, 12800], P('dp', None, 'mp'), may hold values from -80 to 80
- gradient: bfloat16 [8, 5120, 12800], P('dp', None, 'mp'), may hold values from -80 to 80
- right_factor: bfloat16 [12800, 128], P('mp'), may hold values from -6 to 6
Outputs:
- momentum_next: bfloat16 [8, 5120, 12800], P('dp', None, 'mp')
- left_factor: bfloat16 [5120, 128], replicated
- right_next: bfloat16 [12800, 128], P('mp')
All inputs are finite; a program needn't handle non-finite values.
Results may differ from a plain program's by a relative error of at most 0.017.
Values may be sent and summed in bfloat16 or wider, within the bound.
A program may use at most 128 MiB of HBM per device.

v0:
```python
import jax
import jax.numpy as jnp
from jax import lax
from jax.sharding import PartitionSpec as P

D = 5120


DECAY = 0.9


def orthogonal(mean_left, gram):
    lower = jnp.linalg.cholesky(gram)
    return lax.linalg.triangular_solve(
        lower, mean_left, left_side=False, lower=True, transpose_a=True
    )


def shards(momentum, gradient, right_factor):
    blend = (momentum[0].astype(jnp.float32) + gradient[0].astype(jnp.float32)).astype(jnp.bfloat16)
    hid_local = blend.shape[1]
    replicas = lax.axis_size("dp")
    model_size = lax.axis_size("mp")
    root = jnp.sqrt(jnp.float32(D))
    local_left = jnp.dot(blend, right_factor, preferred_element_type=jnp.float32)
    mean_left = lax.psum(local_left, ("dp", "mp")) / replicas
    gram = jnp.dot(mean_left.T, mean_left, precision=lax.Precision.HIGHEST) / D
    left_factor = orthogonal(mean_left, gram).astype(jnp.bfloat16)
    total_rows = hid_local * model_size
    local_right = lax.dot_general(
        blend, left_factor, (((0,), (0,)), ((), ())), preferred_element_type=jnp.float32
    )
    mean_right = lax.psum(local_right.astype(jnp.bfloat16), "dp").astype(jnp.float32) / (
        replicas * root
    )
    squares = lax.psum(jnp.sum(mean_right * mean_right, axis=0), "mp")
    scale = jnp.sqrt(squares / total_rows + 1e-06)
    right_next = (mean_right / scale).astype(jnp.bfloat16)
    right_round = mean_right.astype(jnp.bfloat16)
    coef = (1.0 - DECAY) / root
    low = jnp.dot(left_factor, right_round.T, preferred_element_type=jnp.float32)
    momentum_next = (blend.astype(jnp.float32) - coef * low).astype(jnp.bfloat16)
    return (momentum_next[None], left_factor, right_next)


def solution(mesh):
    placed = (P("dp", None, "mp"), P("dp", None, "mp"), P("mp", None))
    return jax.shard_map(
        shards,
        mesh=mesh,
        in_specs=placed,
        out_specs=(P("dp", None, "mp"), P(), P("mp", None)),
        check_vma=False,
    )
```

profile of v0, /device:TPU:0, one launch (start us, length us, event | category | flops | bytes accessed | tf_op | source)
XLA Modules:
  0.0 333.0 jit_solution(3750027869687122872)
XLA Ops:
  7.2 0.0 copy-start
  7.2 0.0 all-reduce.3.cloned.1.call-start
  7.2 0.9 copy-done
  8.1 10.5 %fusion.20 = f32[5120,128]{1,0:T(8,128)} fusion(bf16[800,128]{1,0:T(8,128)(2,1)S(1)} %copy-done, bf16[1,5120,800]{1,2,0:T(8,128)(2,1)} %param.4, bf16[1,5120,800]{1,2,0:T(8,128)(2,1)} %param.3), kind=kOutput, calls=%fused_computation.30 | convolution fusion | flops 1064960000 | bytes 19210240 | tf_op jit(solution)/shard_map/dot_general | solution.py:25
  18.6 0.0 all-reduce.3.cloned.1.call-update
  18.6 0.2 all-reduce.5.cloned.1.call-start
  18.9 154.0 %all-reduce.3.cloned.1.call-done = f32[5120,128]{1,0:T(8,128)} async-done(((f32[5120,128]{1,0:T(8,128)}), f32[5120,128]{1,0:T(8,128)}) %all-reduce.3.cloned.1.call-update) | async-done | bytes 2621456 | tf_op jit(solution)/shard_map/psum | solution.py:26
  172.8 6.9 %fusion.7 = f32[128,128]{0,1:T(8,128)S(1)} fusion(f32[5120,128]{1,0:T(8,128)} %all-reduce.3.cloned.1.call-done), kind=kOutput, calls=%fused_computation.11 | convolution fusion | flops 1007304704 | bytes 2686976 | tf_op jit(solution)/shard_map/dot_general | solution.py:27
  179.8 0.1 copy.7
  179.9 11.7 %cholesky.16 = f32[128,128]{1,0:T(8,128)S(1)} custom-call(f32[128,128]{1,0:T(8,128)S(1)} %fusion.15), custom_call_target="Cholesky" | custom-call | tf_op jit(solution)/shard_map/jit(cholesky)/cholesky | solution.py:13
  191.6 0.6 compare_reduce_fusion
  192.3 0.7 fusion.13
  192.9 9.8 %custom-call.6 = f32[1,128,128]{1,2,0:T(8,128)S(1)} custom-call(f32[1,128,128]{2,1,0:T(8,128)S(1)} %fusion.13), custom_call_target="InvertDiagBlocksLowerTriangular" | custom-call | tf_op jit(solution)/shard_map/triangular_solve | solution.py:14
  202.8 4.2 %convolution_convert_fusion = bf16[5120,128]{1,0:T(8,128)(2,1)S(1)} fusion(f32[5120,128]{1,0:T(8,128)} %all-reduce.3.cloned.1.call-done, f32[1,128,128]{1,2,0:T(8,128)S(1)} %custom-call.6), kind=kOutput, calls=%fused_computation.4 | convolution fusion | flops 1007943680 | bytes 3997696 | tf_op jit(solution)/shard_map/triangular_solve | solution.py:14
  206.9 0.0 copy-start.1
  207.0 9.1 %convolution_convert_fusion.1 = bf16[800,128]{1,0:T(8,128)(2,1)} fusion(bf16[5120,128]{1,0:T(8,128)(2,1)S(1)} %convolution_convert_fusion, bf16[1,5120,800]{1,2,0:T(8,128)(2,1)} %param.4, bf16[1,5120,800]{1,2,0:T(8,128)(2,1)} %param.3), kind=kOutput, calls=%fused_computation.10 | convolution fusion | flops 1065062400 | bytes 17899520 | tf_op jit(solution)/shard_map/dot_general | solution.py:30
  216.1 0.0 all-reduce.5.cloned.1.call-update
  216.1 56.8 %all-reduce.5.cloned.1.call-done = bf16[800,128]{1,0:T(8,128)(2,1)} async-done(((bf16[800,128]{1,0:T(8,128)(2,1)}), bf16[800,128]{1,0:T(8,128)(2,1)}) %all-reduce.5.cloned.1.call-update) | async-done | bytes 204816 | tf_op jit(solution)/shard_map/psum | solution.py:33
  272.9 1.1 multiply_reduce_fusion
  273.9 40.6 %psum.23 = f32[128]{0:T(128)S(1)} all-reduce(f32[128]{0:T(128)S(1)} %multiply_reduce_fusion), channel_id=1, replica_groups=mesh['dp'=8,'mp'=16] {'mp'}, use_global_device_ids=true, to_apply=%region_5.6 | all-reduce | flops 128 | bytes 1024 | tf_op jit(solution)/shard_map/psum | solution.py:36
  314.6 0.0 copy-done.1
  314.6 0.0 copy-start.2
  314.6 10.8 %fusion.1 = bf16[1,5120,800]{1,2,0:T(8,128)(2,1)} fusion(bf16[5120,128]{1,0:T(8,128)(2,1)S(1)} %convolution_convert_fusion, bf16[800,128]{1,0:T(8,128)(2,1)} %all-reduce.5.cloned.1.call-done, bf16[1,5120,800]{1,2,0:T(8,128)(2,1)} %param.4, bf16[1,5120,800]{1,2,0:T(8,128)(2,1)} %param.3), kind=kOutput, calls=%fused_computation.3 | convolution fusion | flops 1081651200 | bytes 26091520 | tf_op jit(solution)/shard_map/dot_general | solution.py:41
  325.4 0.0 copy-done.2
  325.4 0.7 divide_convert_fusion
  (3 shorter events, 0.1 us)
Async XLA Ops:
  7.2 0.9 copy-start
  7.2 165.7 %all-reduce.3.cloned.1.call-start = ((), (), s32[]{:S(2)}) async-start(), calls=%async_computation | async-start | bytes 5242880 | tf_op jit(solution)/shard_map/psum | solution.py:26
  18.6 254.2 %all-reduce.5.cloned.1.call-start = ((), (), s32[]{:S(2)}) async-start(), calls=%async_computation.1 | async-start | bytes 409600 | tf_op jit(solution)/shard_map/psum | solution.py:33
  206.9 107.6 %copy-start.1 = (bf16[5120,128]{1,0:T(8,128)(2,1)}, bf16[5120,128]{1,0:T(8,128)(2,1)S(1)}, u32[]{:S(2)}) copy-start(bf16[5120,128]{1,0:T(8,128)(2,1)S(1)} %convolution_convert_fusion) | copy-start | bytes 3932164
  314.6 10.8 %copy-start.2 = (bf16[800,128]{1,0:T(8,128)(2,1)S(1)}, bf16[800,128]{1,0:T(8,128)(2,1)}, u32[]{:S(2)}) copy-start(bf16[800,128]{1,0:T(8,128)(2,1)} %all-reduce.5.cloned.1.call-done) | copy-start | bytes 614404
Sparse Core Ops, SparseCore 0:
  18.8 154.0 all-reduce.2
  216.2 56.6 all-reduce.4
where the time goes:
time: 333 us
  waiting for transfers between devices  211 us (63%)
  matrix products  41.6 us (12%)
  blocking collectives  40.6 us (12%)
  other arithmetic  24.7 us (7%)
  between operations  14.1 us (4%)
    psum x1, waiting for transfers between devices, shards(): mean_left = lax.psum(local_left, ('dp', 'mp')) / replicas  154 us
    psum x1, waiting for transfers between devices, shards(): lax.psum(local_right.astype(jnp.bfloat16), 'dp').astype(jnp.float32)  56.8 us
    psum x1, blocking collectives, shards(): squares = lax.psum(jnp.sum(mean_right * mean_right, axis=0), 'mp')  40.6 us
    another operation x3, other arithmetic, orthogonal(): lower = jnp.linalg.cholesky(gram)  12.4 us
    dot_general x1, matrix products, shards(): jnp.dot(left_factor, right_round.T, preferred_element_type=jnp.float32)  10.8 us
    dot_general x1, matrix products, shards(): jnp.dot(blend, right_factor, preferred_element_type=jnp.float32)  10.5 us
    another operation x2, other arithmetic, orthogonal(): lax.linalg.triangular_solve(lower, mean_left, left_side=False, lower=True...  10.5 us
    dot_general x1, matrix products, shards(): lax.dot_general(blend, left_factor, (((0,), (0,)), ((), ())), preferred_e...  9.14 us
  transfers between devices with their start and end apart: 2, of which 2 were waited for; matrix products, arithmetic and copies ran while one was open for 0% of the time, Pallas kernels for 0%

commit v1 on v0

v1 whole, which is shorter than its diff:
```python
import functools
import math

import jax
import jax.numpy as jnp
from jax import lax
from jax.experimental import pallas as pl
from jax.experimental.pallas import tpu as pltpu
from jax.sharding import PartitionSpec as P

D = 5120
RANK = 128
DECAY = 0.9
EPS = 1e-06
MESH = pl.DeviceIdType.MESH
F32 = jnp.float32
BF16 = jnp.bfloat16

CHUNK = 256
N_CHUNKS = D // CHUNK
PARTS = ((0, 8, (0, 1, 2)), (8, 7, (1, 2, 0)), (15, 5, (2, 0, 1)))
STAGES = 7


def device(pos, core):
    return (pos[1] * 2 + core, pos[2] * 4 + pos[0])


def moved(pos, axis, steps):
    at = list(pos)
    at[axis] = lax.rem(pos[axis] + steps, 4)
    return at


def rows_at(start, size):
    return pl.ds(pl.multiple_of(start, 8), size)


def lanes_at(start, size):
    return pl.ds(pl.multiple_of(start, 128), size)


def split(value):
    high = value.astype(BF16)
    return high, (value - high.astype(F32)).astype(BF16)


BLOCK = 4


def eliminate(tiles, k, lane, sub):
    first, shift = k // 8, k % 8
    groups = range(first, RANK // 8)

    def lanes(tile, j):
        return jnp.broadcast_to(tile[:, j : j + 1], (8, RANK))

    def row(tile, i):
        return jnp.broadcast_to(tile[i : i + 1, :], (8, RANK))

    col = [{g: lanes(tiles[g], k + j) for g in groups} for j in range(BLOCK)]
    rows = [row(tiles[first], shift + i) for i in range(BLOCK)]
    piv = [[row(col[j][first], shift + i) for j in range(BLOCK)] for i in range(BLOCK)]
    mult = []
    done = []
    pivots = []
    for j in range(BLOCK):
        inverse = 1.0 / piv[j][j]
        pivots.append(piv[j][j])
        done.append(jnp.where(lane == k + j, 1.0, rows[j]))
        for i in range(j + 1, BLOCK):
            factor = piv[i][j] * inverse
            rows[i] = jnp.where(lane == k + j, 0.0, rows[i]) - factor * done[j]
            for m in range(j + 1, BLOCK):
                piv[i][m] = piv[i][m] - factor * piv[j][m]
        mult.append({g: col[j][g] * inverse for g in groups})
        for m in range(j + 1, BLOCK):
            for g in groups:
                col[m][g] = col[m][g] - mult[j][g] * piv[j][m]
    inside = (lane >= k) & (lane < k + BLOCK)
    last = [
        jnp.where((lane > k + j) & (lane < k + BLOCK), 0.0, done[j]) for j in range(BLOCK)
    ]
    for g in groups:
        new = jnp.where(inside, 0.0, tiles[g])
        for j in range(BLOCK):
            new = new - mult[j][g] * last[j]
        if g == first:
            new = jnp.where(sub < shift + BLOCK, tiles[g], new)
            for j in range(BLOCK):
                new = jnp.where(sub == shift + j, done[j], new)
        tiles[g] = new
    return pivots


def factor_steps(t_ref, root_ref, begin, end):
    lane = lax.broadcasted_iota(jnp.int32, (8, RANK), 1)
    sub = lax.broadcasted_iota(jnp.int32, (8, RANK), 0)
    tiles = [t_ref[8 * g : 8 * g + 8, :] for g in range(RANK // 8)]
    for k in range(begin, end, BLOCK):
        pivots = eliminate(tiles, k, lane, sub)
        for j in range(BLOCK):
            root_ref[k + j : k + j + 1, :] = lax.rsqrt(pivots[j])[0:1, :]
    for g in range(RANK // 8):
        t_ref[8 * g : 8 * g + 8, :] = tiles[g]


def make_kernel(hid, r_rows):
    def kernel(
        mom_hbm, grad_hbm, right_ref,
        blend_hbm, left_hbm, next_ref, round_ref,
        blend, grad, right_t, part_sum, total, pairs, pairs_t, acc_r, acc_g, left_buf,
        from_core, got1, got2, own2, got3,
        r_part, r_core, r_sum, r_y, r_all, t_ref, root_ref, sq_buf,
        load_sem, send_sem, recv_sem, out_sem, r_send, r_recv, sq_send, sq_recv,
    ):
        dp = lax.axis_index("dp")
        mp = lax.axis_index("mp")
        core = lax.rem(dp, 2)
        pos = (lax.rem(mp, 4), dp // 2, mp // 4)
        sibling = device(pos, 1 - core)

        def load(i, what):
            src, dst = ((mom_hbm, blend), (grad_hbm, grad))[what]
            return pltpu.make_async_copy(
                src.at[0, :, lanes_at(i * CHUNK, CHUNK)],
                dst.at[:, lanes_at(i * CHUNK, CHUNK)],
                load_sem.at[what, i],
            )

        def start_load(i, _):
            load(i, 0).start()
            load(i, 1).start()
            return 0

        lax.fori_loop(0, N_CHUNKS, start_load, 0)

        right_t[...] = right_ref[...].astype(F32).T.astype(BF16)
        barrier = pltpu.get_barrier_semaphore()
        greet = [sibling]
        greet += [device(moved(pos, a, r), core) for a in range(3) for r in range(1, 4)]
        greet += [
            device(moved(moved(pos, 0, r), 2, s), core) for r in range(1, 4) for s in range(1, 4)
        ]
        for peer in greet:
            pl.semaphore_signal(barrier, inc=1, device_id=peer, device_id_type=MESH)

        def remote(src, dst, send, recv, peer):
            return pltpu.make_async_remote_copy(
                src_ref=src, dst_ref=dst, send_sem=send, recv_sem=recv,
                device_id=peer, device_id_type=MESH,
            )

        def took(ref, sem):
            pltpu.make_async_copy(ref, ref, sem).wait()

        def left_chunks(begin, end):
            def one(i, _):
                load(i, 0).wait()
                load(i, 1).wait()
                at = lanes_at(i * CHUNK, CHUNK)
                value = (blend[:, at].astype(F32) + grad[:, at].astype(F32)).astype(BF16)
                blend[:, at] = value
                terms = jnp.dot(right_t[...], value, preferred_element_type=F32)
                for t in range(CHUNK // 128):
                    rows = rows_at(i * CHUNK + t * 128, 128)
                    part_sum[rows, :] = terms[:, t * 128 : (t + 1) * 128]
                return 0

            lax.fori_loop(begin, end, one, 0)

        def geometry(p):
            begin, chunks, axes = PARTS[p]
            half = chunks * CHUNK // 2
            base = begin * CHUNK
            own = base + core * half
            quarter = half // 4
            small = quarter // 4
            return base, half, own, quarter, small, axes

        def core_send(p):
            base, half, own, quarter, small, axes = geometry(p)
            other = base + (1 - core) * half
            remote(
                part_sum.at[rows_at(other, half)], from_core.at[pl.ds(base // 2, half)],
                send_sem.at[p, 0], recv_sem.at[p, 0], sibling,
            ).start()

        def axis_send(p):
            base, half, own, quarter, small, axes = geometry(p)
            took(from_core.at[pl.ds(base // 2, half)], recv_sem.at[p, 0])
            step = 128
            for r in range(0, half, step):
                size = min(step, half - r)
                part_sum[rows_at(own + r, size), :] += from_core[pl.ds(base // 2 + r, size), :]
            for r in range(1, 4):
                to = lax.rem(pos[axes[0]] + r, 4)
                remote(
                    part_sum.at[rows_at(own + to * quarter, quarter)],
                    got1.at[r - 1, pl.ds(base // 8, quarter)],
                    send_sem.at[p, 1], recv_sem.at[p, 1], device(moved(pos, axes[0], r), core),
                ).start()

        def second_send(p):
            base, half, own, quarter, small, axes = geometry(p)
            here = pl.ds(base // 8, quarter)
            took(got1.at[:, here], recv_sem.at[p, 1])
            mine = rows_at(own + pos[axes[0]] * quarter, quarter)
            got1[0, here, :] = (part_sum[mine, :] + got1[0, here, :]) + (
                got1[1, here, :] + got1[2, here, :]
            )
            for r in range(1, 4):
                to = lax.rem(pos[axes[1]] + r, 4)
                remote(
                    got1.at[0, rows_at(base // 8 + to * small, small)],
                    got2.at[r - 1, pl.ds(base // 32, small)],
                    send_sem.at[p, 2], recv_sem.at[p, 2], device(moved(pos, axes[1], r), core),
                ).start()

        def third_send(p):
            base, half, own, quarter, small, axes = geometry(p)
            here = pl.ds(base // 32, small)
            took(got2.at[:, here], recv_sem.at[p, 2])
            mine = rows_at(base // 8 + pos[axes[1]] * small, small)
            own2[here, :] = (got1[0, mine, :] + got2[0, here, :]) + (
                got2[1, here, :] + got2[2, here, :]
            )
            me = pos[axes[2]]
            for r in range(1, 4):
                remote(
                    own2.at[here],
                    got3.at[r - 1, here],
                    send_sem.at[p, 3], recv_sem.at[p, 3], device(moved(pos, axes[2], r), core),
                ).start()

        def gather_send(p):
            base, half, own, quarter, small, axes = geometry(p)
            here = pl.ds(base // 32, small)
            took(got3.at[:, here], recv_sem.at[p, 3])
            me = pos[axes[2]]
            terms = [own2[here, :]] + [got3[r, here, :] for r in range(3)]

            def at_place(j):
                value = terms[0]
                for r in range(1, 4):
                    value = jnp.where(lax.rem(me + 4 - r, 4) == j, terms[r], value)
                return value

            mine = rows_at(own + pos[axes[0]] * quarter + pos[axes[1]] * small, small)
            total[mine, :] = (at_place(0) + at_place(1)) + (at_place(2) + at_place(3))
            for r in range(1, 4):
                remote(
                    total.at[mine], total.at[mine],
                    send_sem.at[p, 4], recv_sem.at[p, 4], device(moved(pos, axes[1], r), core),
                ).start()

        def gather_axis(p):
            base, half, own, quarter, small, axes = geometry(p)
            took(total.at[pl.ds(0, 3 * small)], recv_sem.at[p, 4])
            mine = rows_at(own + pos[axes[0]] * quarter, quarter)
            for r in range(1, 4):
                remote(
                    total.at[mine], total.at[mine],
                    send_sem.at[p, 5], recv_sem.at[p, 5], device(moved(pos, axes[0], r), core),
                ).start()

        def gather_core(p):
            base, half, own, quarter, small, axes = geometry(p)
            took(total.at[pl.ds(0, 3 * quarter)], recv_sem.at[p, 5])
            mine = rows_at(own, half)
            remote(
                total.at[mine], total.at[mine], send_sem.at[p, 6], recv_sem.at[p, 6], sibling
            ).start()

        def use_part(p):
            base, half, own, quarter, small, axes = geometry(p)
            took(total.at[pl.ds(0, half)], recv_sem.at[p, 6])
            size = 2 * half

            def one(i, _):
                at = rows_at(base + i * 128, 128)
                value = total[at, :]
                high, low = split(value)
                cols = lanes_at(i * 128, 128)
                pairs_t[0:RANK, cols] = high
                pairs_t[RANK : 2 * RANK, cols] = low
                high, low = split(value.T)
                pairs[at, 0:RANK] = high
                pairs[at, RANK : 2 * RANK] = low
                return 0

            lax.fori_loop(0, size // 128, one, 0)
            rows = pl.ds(base, size)
            terms = pairs[rows, :]
            gram = jnp.dot(pairs_t[:, 0:size], terms, preferred_element_type=F32)
            acc_g[...] = gram if p == 0 else acc_g[...] + gram
            value = jnp.dot(blend[:, rows], terms, preferred_element_type=F32)
            acc_r[...] = value if p == 0 else acc_r[...] + value

        def sent(p):
            base, half, own, quarter, small, axes = geometry(p)
            took(total.at[pl.ds(0, half)], send_sem.at[p, 0])
            took(total.at[pl.ds(0, 3 * quarter)], send_sem.at[p, 1])
            took(total.at[pl.ds(0, 3 * small)], send_sem.at[p, 2])
            took(total.at[pl.ds(0, 3 * small)], send_sem.at[p, 3])
            took(total.at[pl.ds(0, 3 * small)], send_sem.at[p, 4])
            took(total.at[pl.ds(0, 3 * quarter)], send_sem.at[p, 5])
            took(total.at[pl.ds(0, half)], send_sem.at[p, 6])

        with jax.named_scope("left_product"):
            left_chunks(0, 8)
        with jax.named_scope("barrier"):
            pl.semaphore_wait(barrier, len(greet))
        core_send(0)
        with jax.named_scope("left_product"):
            left_chunks(8, 12)
        axis_send(0)
        with jax.named_scope("left_product"):
            left_chunks(12, 15)
        core_send(1)
        with jax.named_scope("left_product"):
            left_chunks(15, 18)
        axis_send(1)
        with jax.named_scope("left_product"):
            left_chunks(18, 20)
        core_send(2)
        keep = pltpu.make_async_copy(blend, blend_hbm, out_sem.at[0])
        keep.start()
        with jax.named_scope("axis_send"):
            axis_send(2)
        for name, stage in (
            ("second_send", second_send), ("third_send", third_send),
            ("gather_send", gather_send), ("gather_axis", gather_axis),
        ):
            for p in range(3):
                with jax.named_scope(name + str(p)):
                    stage(p)
        with jax.named_scope("gather_core"):
            gather_core(0)
            gather_core(1)
        with jax.named_scope("use_part0"):
            use_part(0)
        with jax.named_scope("gather_core2"):
            gather_core(2)
        with jax.named_scope("use_part1"):
            use_part(1)
        with jax.named_scope("use_part2"):
            use_part(2)

        r_part[0:hid, :] = acc_r[:, 0:RANK] + acc_r[:, RANK : 2 * RANK]
        r_part[hid:, :] = jnp.zeros((r_rows - hid, RANK), F32)
        half_rows = r_rows // 2
        remote(
            r_part.at[rows_at((1 - core) * half_rows, half_rows)], r_core,
            r_send.at[0], r_recv.at[0], sibling,
        ).start()
        t_ref[...] = (acc_g[0:RANK, 0:RANK] + acc_g[RANK:, 0:RANK]) + (
            acc_g[0:RANK, RANK:] + acc_g[RANK:, RANK:]
        )
        with jax.named_scope("factor_steps0"):
            factor_steps(t_ref, root_ref, 0, 16)
        with jax.named_scope("r_core_wait"):
            took(r_core, r_recv.at[0])
        own_half = rows_at(core * half_rows, half_rows)
        r_sum[...] = r_part[own_half, :] + r_core[...]
        piece = half_rows // 4
        for r in range(1, 4):
            to = lax.rem(pos[1] + r, 4)
            remote(
                r_sum.at[rows_at(to * piece, piece)], r_y.at[r - 1],
                r_send.at[1], r_recv.at[1], device(moved(pos, 1, r), core),
            ).start()
        with jax.named_scope("factor_steps16"):
            factor_steps(t_ref, root_ref, 16, 56)
        with jax.named_scope("r_y_wait"):
            took(r_y, r_recv.at[1])
        took(r_core, r_send.at[0])
        mine = rows_at(core * half_rows + pos[1] * piece, piece)
        r_all[mine, :] = (r_sum[rows_at(pos[1] * piece, piece), :] + r_y[0]) + (r_y[1] + r_y[2])
        for r in range(1, 4):
            remote(
                r_all.at[mine], r_all.at[mine],
                r_send.at[2], r_recv.at[2], device(moved(pos, 1, r), core),
            ).start()
        with jax.named_scope("factor_steps56"):
            factor_steps(t_ref, root_ref, 56, 96)
        with jax.named_scope("r_y_gather_wait"):
            took(r_y, r_recv.at[2])
        remote(
            r_all.at[own_half], r_all.at[own_half], r_send.at[3], r_recv.at[3], sibling
        ).start()
        with jax.named_scope("factor_steps96"):
            factor_steps(t_ref, root_ref, 96, RANK)
        lane = lax.broadcasted_iota(jnp.int32, (RANK, RANK), 1)
        sub = lax.broadcasted_iota(jnp.int32, (RANK, RANK), 0)
        lower = jnp.where(lane < sub, t_ref[...], jnp.where(lane == sub, 1.0, 0.0)) * root_ref[...]
        with jax.named_scope("r_core_gather_wait"):
            took(r_core, r_recv.at[3])
        lower_t = lower.T
        mean = jnp.dot(
            r_all[0:hid, :], lower_t, precision=lax.Precision.HIGHEST, preferred_element_type=F32
        ) * F32(0.125)
        round_ref[...] = mean.astype(BF16)
        squares = jnp.broadcast_to(jnp.sum(mean * mean, axis=0, keepdims=True), (8, RANK))
        sq_buf[mp] = squares
        for s in range(4):
            for r in range(4):
                if r or s:
                    remote(
                        sq_buf.at[mp], sq_buf.at[mp], sq_send.at[0], sq_recv.at[0],
                        device(moved(moved(pos, 0, r), 2, s), core),
                    ).start()

        high, low = split(lower_t)
        both = jnp.concatenate([high, low], axis=1)
        weights = jnp.concatenate([both, both], axis=0)
        root = F32(math.sqrt(D))

        def left_rows(i, _):
            at = rows_at(i * CHUNK, CHUNK)
            value = jnp.dot(pairs[at, :], weights, preferred_element_type=F32)
            left_buf[at, :] = ((value[:, :RANK] + value[:, RANK:]) * root).astype(BF16)
            return 0

        with jax.named_scope("left_rows"):
            lax.fori_loop(0, N_CHUNKS, left_rows, 0)
        left_out = pltpu.make_async_copy(left_buf, left_hbm, out_sem.at[1])
        left_out.start()
        with jax.named_scope("squares_wait"):
            took(sq_buf.at[pl.ds(0, 15)], sq_recv.at[0])
        all_squares = sq_buf[0]
        for i in range(1, 16):
            all_squares = all_squares + sq_buf[i]
        scale = jnp.sqrt(all_squares[0:1, :] / (hid * 16) + EPS)
        next_ref[...] = (mean / scale).astype(BF16)

        took(sq_buf.at[pl.ds(0, 15)], sq_send.at[0])
        took(r_y, r_send.at[1])
        took(r_y, r_send.at[2])
        took(r_core, r_send.at[3])
        for p in range(3):
            sent(p)
        left_out.wait()
        keep.wait()

    return kernel


def factors(momentum, gradient, right_factor):
    hid = momentum.shape[1]
    r_rows = -(-hid // 64) * 64
    vmem = pl.BlockSpec(memory_space=pltpu.VMEM)
    hbm = pl.BlockSpec(memory_space=pl.ANY)
    return pl.pallas_call(
        make_kernel(hid, r_rows),
        out_shape=(
            jax.ShapeDtypeStruct((hid, D), BF16),
            jax.ShapeDtypeStruct((D, RANK), BF16),
            jax.ShapeDtypeStruct((hid, RANK), BF16),
            jax.ShapeDtypeStruct((hid, RANK), BF16),
        ),
        in_specs=[hbm, hbm, vmem],
        out_specs=(hbm, hbm, vmem, vmem),
        scratch_shapes=[
            pltpu.VMEM((hid, D), BF16),
            pltpu.VMEM((hid, D), BF16),
            pltpu.VMEM((RANK, hid), BF16),
            pltpu.VMEM((D, RANK), F32),
            pltpu.VMEM((D, RANK), F32),
            pltpu.VMEM((D, 2 * RANK), BF16),
            pltpu.VMEM((2 * RANK, 8 * CHUNK), BF16),
            pltpu.VMEM((hid, 2 * RANK), F32),
            pltpu.VMEM((2 * RANK, 2 * RANK), F32),
            pltpu.VMEM((D, RANK), BF16),
            pltpu.VMEM((D // 2, RANK), F32),
            pltpu.VMEM((3, D // 8, RANK), F32),
            pltpu.VMEM((3, D // 32, RANK), F32),
            pltpu.VMEM((D // 32, RANK), F32),
            pltpu.VMEM((3, D // 32, RANK), F32),
            pltpu.VMEM((r_rows, RANK), F32),
            pltpu.VMEM((r_rows // 2, RANK), F32),
            pltpu.VMEM((r_rows // 2, RANK), F32),
            pltpu.VMEM((3, r_rows // 8, RANK), F32),
            pltpu.VMEM((r_rows, RANK), F32),
            pltpu.VMEM((RANK, RANK), F32),
            pltpu.VMEM((RANK, RANK), F32),
            pltpu.VMEM((16, 8, RANK), F32),
            pltpu.SemaphoreType.DMA((2, N_CHUNKS)),
            pltpu.SemaphoreType.DMA((3, STAGES)),
            pltpu.SemaphoreType.DMA((3, STAGES)),
            pltpu.SemaphoreType.DMA((2,)),
            pltpu.SemaphoreType.DMA((4,)),
            pltpu.SemaphoreType.DMA((4,)),
            pltpu.SemaphoreType.DMA((1,)),
            pltpu.SemaphoreType.DMA((1,)),
        ],
        compiler_params=pltpu.CompilerParams(
            collective_id=0, has_side_effects=True, vmem_limit_bytes=60 << 20
        ),
        name="factors",
    )(momentum, gradient, right_factor)


def feedback_kernel(blend_ref, left_ref, round_ref, out_ref):
    low = lax.dot_general(
        round_ref[...], left_ref[...], (((1,), (1,)), ((), ())), preferred_element_type=F32
    )
    coef = F32((1.0 - DECAY) / math.sqrt(D))
    out_ref[0] = (blend_ref[...].astype(F32) - coef * low).astype(BF16)


def feedback(blend, left_factor, right_round):
    hid = blend.shape[0]
    cols = 512
    return pl.pallas_call(
        feedback_kernel,
        grid=(D // cols,),
        out_shape=jax.ShapeDtypeStruct((1, hid, D), BF16),
        in_specs=[
            pl.BlockSpec((hid, cols), lambda i: (0, i)),
            pl.BlockSpec((cols, RANK), lambda i: (i, 0)),
            pl.BlockSpec((hid, RANK), lambda i: (0, 0)),
        ],
        out_specs=pl.BlockSpec((1, hid, cols), lambda i: (0, 0, i)),
        compiler_params=pltpu.CompilerParams(vmem_limit_bytes=60 << 20),
        name="feedback",
    )(blend, left_factor, right_round)


def shards(momentum, gradient, right_factor):
    blend, left_factor, right_next, right_round = factors(
        momentum.swapaxes(1, 2), gradient.swapaxes(1, 2), right_factor
    )
    momentum_next = feedback(blend, left_factor, right_round).swapaxes(1, 2)
    return momentum_next, left_factor, right_next


def solution(mesh):
    placed = (P("dp", None, "mp"), P("dp", None, "mp"), P("mp", None))
    return jax.shard_map(
        shards,
        mesh=mesh,
        in_specs=placed,
        out_specs=(P("dp", None, "mp"), P(), P("mp", None)),
        check_vma=False,
    )
```

time: 333 us -> 82.8 us (0.25)
  waiting for transfers between devices: 211 us -> 0 us
  Pallas kernels: 0 us -> 79.3 us
  matrix products: 41.6 us -> 0 us
  blocking collectives: 40.6 us -> 0 us
  other arithmetic: 24.7 us -> 0 us
  between operations: 14.1 us -> 0.66 us
    psum x2 -> x0, waiting for transfers between devices: 211 us -> none  [the longest x1 154 us: shards(): mean_left = lax.psum(local_left, ('dp', 'mp')) / replicas]
    pallas_call x0 -> x2, Pallas kernels: none -> 79.3 us  [the longest x1 67.4 us: factors(): pl.pallas_call(make_kernel(hid, r_rows), out_shape=(jax.ShapeDtypeStruct(...]
    psum x1 -> x0, blocking collectives: 40.6 us -> none  [shards(): squares = lax.psum(jnp.sum(mean_right * mean_right, axis=0), 'mp')]
    dot_general x4 -> x0, matrix products: 37.4 us -> none  [the longest x1 10.8 us: shards(): jnp.dot(left_factor, right_round.T, preferred_element_type=jnp.float32)]
    another operation x5 -> x0, other arithmetic: 22.9 us -> none  [the longest x3 12.4 us: orthogonal(): lower = jnp.linalg.cholesky(gram)]
    another operation x1 -> x0, matrix products: 4.18 us -> none  [orthogonal(): lax.linalg.triangular_solve(lower, mean_left, left_side=False, lower=True...]
  transfers between devices with their start and end apart: 2 -> 0, of which waited for: 2 -> 0; matrix products, arithmetic and copies ran while one was open for 0% -> 0% of each run, Pallas kernels for 0% -> 0%
where the time goes in v1:
time: 82.8 us; the launch traced here: 81.7 us
  Pallas kernels  79.3 us (96%)
  local copies, waits for them, and re-layouts  1.74 us (2%)
    pallas_call x1, Pallas kernels, factors(): pl.pallas_call(make_kernel(hid, r_rows), out_shape=(jax.ShapeDtypeStruct(...  67.4 us
    pallas_call x1, Pallas kernels, feedback(): pl.pallas_call(feedback_kernel, grid=(D // cols,), out_shape=jax.ShapeDty...  11.9 us
    unnamed x6, local copies, waits for them, and re-layouts  1.74 us

profile of v1, /device:TPU:0, one launch (start us, length us, event | category | flops | bytes accessed | tf_op | source)
XLA Modules:
  0.0 81.7 jit_solution(126497620639688097)
XLA Ops:
  0.6 67.4 %factors.1 = (bf16[800,5120]{1,0:T(8,128)(2,1)}, bf16[5120,128]{1,0:T(8,128)(2,1)}, bf16[800,128]{1,0:T(8,128)(2,1)}, bf16[800,128]{1,0:T(8,128)(2,1)}) custom-call(bf16[1,800,5120]{2,1,0:T(8,128)(2,1)} %bitcast.3, bf16[1,800,5120]{2,1,0:T(8,128)(2,1)} %bitcast.4, bf16[800,128]{1,0:T(8,128)(2,1)} %right_ref.1), custom_call_target="tpu_custom_call" | custom-call | tf_op jit(solution)/shard_map/factors/pallas_call | solution.py:454
  68.1 0.0 copy-start
  68.1 0.0 copy-start.1
  68.1 11.9 %feedback.1 = bf16[1,800,5120]{2,1,0:T(8,128)(2,1)} custom-call(bf16[800,5120]{1,0:T(8,128)(2,1)} %get-tuple-element.7.blend_ref, bf16[5120,128]{1,0:T(8,128)(2,1)} %get-tuple-element.15.left_ref, bf16[800,128]{1,0:T(8,128)(2,1)} %get-tuple-element.9.round_ref), custom_call_target="tpu_custom_call" | custom-call | tf_op jit(solution)/shard_map/feedback/pallas_call | solution.py:515
  80.0 0.0 copy-done
  80.0 1.1 %copy.8 = bf16[5120,128]{1,0:T(8,128)(2,1)} copy(bf16[5120,128]{1,0:T(8,128)(2,1)S(1)} %copy-done) | data formatting | bytes 2621440
  81.0 0.0 copy-done.1
  81.0 0.7 copy.9
Async XLA Ops:
  68.1 11.9 %copy-start = (bf16[5120,128]{1,0:T(8,128)(2,1)S(1)}, bf16[5120,128]{1,0:T(8,128)(2,1)}, u32[]{:S(2)}) copy-start(bf16[5120,128]{1,0:T(8,128)(2,1)} %get-tuple-element.15.left_ref) | copy-start | bytes 3932164
  68.1 12.9 %copy-start.1 = (bf16[800,128]{1,0:T(8,128)(2,1)S(1)}, bf16[800,128]{1,0:T(8,128)(2,1)}, u32[]{:S(2)}) copy-start(bf16[800,128]{1,0:T(8,128)(2,1)} %get-tuple-element.16) | copy-start | bytes 614404

commit v2 on v1

--- a/solution.py
+++ b/solution.py
@@ -15,10 +15,11 @@
 MESH = pl.DeviceIdType.MESH
 F32 = jnp.float32
 BF16 = jnp.bfloat16
-
-CHUNK = 256
+NT = (((1,), (1,)), ((), ()))
+
+CHUNK = 512
 N_CHUNKS = D // CHUNK
-PARTS = ((0, 8, (0, 1, 2)), (8, 7, (1, 2, 0)), (15, 5, (2, 0, 1)))
+PARTS = ((0, 4, (0, 1, 2)), (4, 3, (1, 2, 0)), (7, 3, (2, 0, 1)))
 STAGES = 7
 
 
@@ -40,12 +41,16 @@
     return pl.ds(pl.multiple_of(start, 128), size)
 
 
+def rows_at16(start, size):
+    return pl.ds(pl.multiple_of(start, 16), size)
+
+
 def split(value):
     high = value.astype(BF16)
     return high, (value - high.astype(F32)).astype(BF16)
 
 
-BLOCK = 4
+BLOCK = 8
 
 
 def eliminate(tiles, k, lane, sub):
@@ -107,18 +112,19 @@
 
 def make_kernel(hid, r_rows):
     def kernel(
-        mom_hbm, grad_hbm, right_ref,
-        blend_hbm, left_hbm, next_ref, round_ref,
-        blend, grad, right_t, part_sum, total, pairs, pairs_t, acc_r, acc_g, left_buf,
+        mom_hbm, grad_hbm, right_hbm,
+        out_ref, left_ref, next_ref,
+        grad, right_in, right_t, part_sum, total, pairs_t, left_t, acc_r, acc_g,
         from_core, got1, got2, own2, got3,
-        r_part, r_core, r_sum, r_y, r_all, t_ref, root_ref, sq_buf,
-        load_sem, send_sem, recv_sem, out_sem, r_send, r_recv, sq_send, sq_recv,
+        r_part, r_core, r_sum, r_y, r_all, t_ref, root_ref, sq_buf, sq_dp,
+        load_sem, right_sem, send_sem, recv_sem, r_send, r_recv, sq_send, sq_recv,
     ):
         dp = lax.axis_index("dp")
         mp = lax.axis_index("mp")
         core = lax.rem(dp, 2)
         pos = (lax.rem(mp, 4), dp // 2, mp // 4)
         sibling = device(pos, 1 - core)
+        blend = out_ref.at[0]
 
         def load(i, what):
             src, dst = ((mom_hbm, blend), (grad_hbm, grad))[what]
@@ -128,22 +134,23 @@
                 load_sem.at[what, i],
             )
 
-        def start_load(i, _):
+        right_load = pltpu.make_async_copy(right_hbm, right_in, right_sem.at[0])
+        right_load.start()
+        for i in range(N_CHUNKS):
             load(i, 0).start()
             load(i, 1).start()
-            return 0
-
-        lax.fori_loop(0, N_CHUNKS, start_load, 0)
-
-        right_t[...] = right_ref[...].astype(F32).T.astype(BF16)
+
         barrier = pltpu.get_barrier_semaphore()
         greet = [sibling]
         greet += [device(moved(pos, a, r), core) for a in range(3) for r in range(1, 4)]
+        greet += [device(moved(pos, 1, r), 1 - core) for r in range(1, 4)]
         greet += [
             device(moved(moved(pos, 0, r), 2, s), core) for r in range(1, 4) for s in range(1, 4)
         ]
         for peer in greet:
             pl.semaphore_signal(barrier, inc=1, device_id=peer, device_id_type=MESH)
+        right_load.wait()
+        right_t[...] = right_in[...].astype(F32).T.astype(BF16)
 
         def remote(src, dst, send, recv, peer):
             return pltpu.make_async_remote_copy(
@@ -272,30 +279,24 @@
                 total.at[mine], total.at[mine], send_sem.at[p, 6], recv_sem.at[p, 6], sibling
             ).start()
 
-        def use_part(p):
-            base, half, own, quarter, small, axes = geometry(p)
-            took(total.at[pl.ds(0, half)], recv_sem.at[p, 6])
-            size = 2 * half
-
-            def one(i, _):
-                at = rows_at(base + i * 128, 128)
-                value = total[at, :]
-                high, low = split(value)
-                cols = lanes_at(i * 128, 128)
+        def use_half(p, which, first=False):
+            base, half, own, quarter, small, axes = geometry(p)
+            start = own
+            if which:
+                took(total.at[pl.ds(0, half)], recv_sem.at[p, 6])
+                start = base + (1 - core) * half
+
+            for t in range(half // 128):
+                high, low = split(total[rows_at(start + t * 128, 128), :])
+                cols = lanes_at(start + t * 128, 128)
                 pairs_t[0:RANK, cols] = high
                 pairs_t[RANK : 2 * RANK, cols] = low
-                high, low = split(value.T)
-                pairs[at, 0:RANK] = high
-                pairs[at, RANK : 2 * RANK] = low
-                return 0
-
-            lax.fori_loop(0, size // 128, one, 0)
-            rows = pl.ds(base, size)
-            terms = pairs[rows, :]
-            gram = jnp.dot(pairs_t[:, 0:size], terms, preferred_element_type=F32)
-            acc_g[...] = gram if p == 0 else acc_g[...] + gram
-            value = jnp.dot(blend[:, rows], terms, preferred_element_type=F32)
-            acc_r[...] = value if p == 0 else acc_r[...] + value
+            cols = lanes_at(start, half)
+            terms = pairs_t[:, cols]
+            gram = lax.dot_general(terms, terms, NT, preferred_element_type=F32)
+            acc_g[...] = gram if first else acc_g[...] + gram
+            value = lax.dot_general(blend[:, cols], terms, NT, preferred_element_type=F32)
+            acc_r[...] = value if first else acc_r[...] + value
 
         def sent(p):
             base, half, own, quarter, small, axes = geometry(p)
@@ -307,45 +308,35 @@
             took(total.at[pl.ds(0, 3 * quarter)], send_sem.at[p, 5])
             took(total.at[pl.ds(0, half)], send_sem.at[p, 6])
 
-        with jax.named_scope("left_product"):
-            left_chunks(0, 8)
-        with jax.named_scope("barrier"):
-            pl.semaphore_wait(barrier, len(greet))
+        left_chunks(0, 4)
+        pl.semaphore_wait(barrier, len(greet))
         core_send(0)
-        with jax.named_scope("left_product"):
-            left_chunks(8, 12)
+        left_chunks(4, 6)
         axis_send(0)
-        with jax.named_scope("left_product"):
-            left_chunks(12, 15)
+        left_chunks(6, 7)
         core_send(1)
-        with jax.named_scope("left_product"):
-            left_chunks(15, 18)
+        left_chunks(7, 9)
         axis_send(1)
-        with jax.named_scope("left_product"):
-            left_chunks(18, 20)
+        left_chunks(9, 10)
         core_send(2)
-        keep = pltpu.make_async_copy(blend, blend_hbm, out_sem.at[0])
-        keep.start()
-        with jax.named_scope("axis_send"):
-            axis_send(2)
-        for name, stage in (
-            ("second_send", second_send), ("third_send", third_send),
-            ("gather_send", gather_send), ("gather_axis", gather_axis),
-        ):
-            for p in range(3):
-                with jax.named_scope(name + str(p)):
-                    stage(p)
-        with jax.named_scope("gather_core"):
-            gather_core(0)
-            gather_core(1)
-        with jax.named_scope("use_part0"):
-            use_part(0)
-        with jax.named_scope("gather_core2"):
-            gather_core(2)
-        with jax.named_scope("use_part1"):
-            use_part(1)
-        with jax.named_scope("use_part2"):
-            use_part(2)
+        axis_send(2)
+        for p in range(3):
+            second_send(p)
+        for p in range(3):
+            third_send(p)
+        for p in range(3):
+            gather_send(p)
+        for p in range(3):
+            gather_axis(p)
+        gather_core(0)
+        gather_core(1)
+        use_half(0, 0, first=True)
+        use_half(1, 0)
+        gather_core(2)
+        use_half(0, 1)
+        use_half(1, 1)
+        use_half(2, 0)
+        use_half(2, 1)
 
         r_part[0:hid, :] = acc_r[:, 0:RANK] + acc_r[:, RANK : 2 * RANK]
         r_part[hid:, :] = jnp.zeros((r_rows - hid, RANK), F32)
@@ -357,10 +348,8 @@
         t_ref[...] = (acc_g[0:RANK, 0:RANK] + acc_g[RANK:, 0:RANK]) + (
             acc_g[0:RANK, RANK:] + acc_g[RANK:, RANK:]
         )
-        with jax.named_scope("factor_steps0"):
-            factor_steps(t_ref, root_ref, 0, 16)
-        with jax.named_scope("r_core_wait"):
-            took(r_core, r_recv.at[0])
+        factor_steps(t_ref, root_ref, 0, 16)
+        took(r_core, r_recv.at[0])
         own_half = rows_at(core * half_rows, half_rows)
         r_sum[...] = r_part[own_half, :] + r_core[...]
         piece = half_rows // 4
@@ -370,39 +359,23 @@
                 r_sum.at[rows_at(to * piece, piece)], r_y.at[r - 1],
                 r_send.at[1], r_recv.at[1], device(moved(pos, 1, r), core),
             ).start()
-        with jax.named_scope("factor_steps16"):
-            factor_steps(t_ref, root_ref, 16, 56)
-        with jax.named_scope("r_y_wait"):
-            took(r_y, r_recv.at[1])
-        took(r_core, r_send.at[0])
-        mine = rows_at(core * half_rows + pos[1] * piece, piece)
-        r_all[mine, :] = (r_sum[rows_at(pos[1] * piece, piece), :] + r_y[0]) + (r_y[1] + r_y[2])
+        factor_steps(t_ref, root_ref, 16, RANK)
+        lane = lax.broadcasted_iota(jnp.int32, (RANK, RANK), 1)
+        sub = lax.broadcasted_iota(jnp.int32, (RANK, RANK), 0)
+        lower = jnp.where(lane < sub, t_ref[...], jnp.where(lane == sub, 1.0, 0.0)) * root_ref[...]
+        took(r_y, r_recv.at[1])
+        summed = (r_sum[rows_at(pos[1] * piece, piece), :] + r_y[0]) + (r_y[1] + r_y[2])
+        mean = lax.dot_general(
+            summed, lower, NT, precision=lax.Precision.HIGHEST, preferred_element_type=F32
+        ) * F32(0.125)
+        mine = rows_at16(core * half_rows + pos[1] * piece, piece)
+        r_all[mine, :] = mean.astype(BF16)
         for r in range(1, 4):
             remote(
                 r_all.at[mine], r_all.at[mine],
                 r_send.at[2], r_recv.at[2], device(moved(pos, 1, r), core),
             ).start()
-        with jax.named_scope("factor_steps56"):
-            factor_steps(t_ref, root_ref, 56, 96)
-        with jax.named_scope("r_y_gather_wait"):
-            took(r_y, r_recv.at[2])
-        remote(
-            r_all.at[own_half], r_all.at[own_half], r_send.at[3], r_recv.at[3], sibling
-        ).start()
-        with jax.named_scope("factor_steps96"):
-            factor_steps(t_ref, root_ref, 96, RANK)
-        lane = lax.broadcasted_iota(jnp.int32, (RANK, RANK), 1)
-        sub = lax.broadcasted_iota(jnp.int32, (RANK, RANK), 0)
-        lower = jnp.where(lane < sub, t_ref[...], jnp.where(lane == sub, 1.0, 0.0)) * root_ref[...]
-        with jax.named_scope("r_core_gather_wait"):
-            took(r_core, r_recv.at[3])
-        lower_t = lower.T
-        mean = jnp.dot(
-            r_all[0:hid, :], lower_t, precision=lax.Precision.HIGHEST, preferred_element_type=F32
-        ) * F32(0.125)
-        round_ref[...] = mean.astype(BF16)
-        squares = jnp.broadcast_to(jnp.sum(mean * mean, axis=0, keepdims=True), (8, RANK))
-        sq_buf[mp] = squares
+        sq_buf[mp] = jnp.broadcast_to(jnp.sum(mean * mean, axis=0, keepdims=True), (8, RANK))
         for s in range(4):
             for r in range(4):
                 if r or s:
@@ -411,67 +384,84 @@
                         device(moved(moved(pos, 0, r), 2, s), core),
                     ).start()
 
-        high, low = split(lower_t)
-        both = jnp.concatenate([high, low], axis=1)
-        weights = jnp.concatenate([both, both], axis=0)
+        high, low = split(lower)
+        weights = jnp.concatenate(
+            [jnp.concatenate([high, high], axis=1), jnp.concatenate([low, low], axis=1)], axis=0
+        )
         root = F32(math.sqrt(D))
 
-        def left_rows(i, _):
-            at = rows_at(i * CHUNK, CHUNK)
-            value = jnp.dot(pairs[at, :], weights, preferred_element_type=F32)
-            left_buf[at, :] = ((value[:, :RANK] + value[:, RANK:]) * root).astype(BF16)
-            return 0
-
-        with jax.named_scope("left_rows"):
-            lax.fori_loop(0, N_CHUNKS, left_rows, 0)
-        left_out = pltpu.make_async_copy(left_buf, left_hbm, out_sem.at[1])
-        left_out.start()
-        with jax.named_scope("squares_wait"):
-            took(sq_buf.at[pl.ds(0, 15)], sq_recv.at[0])
-        all_squares = sq_buf[0]
+        for i in range(N_CHUNKS):
+            at = slice(i * CHUNK, (i + 1) * CHUNK)
+            value = jnp.dot(weights, pairs_t[:, at], preferred_element_type=F32)
+            value = (value[:RANK, :] + value[RANK:, :]) * root
+            left_t[:, at] = value.astype(BF16)
+            left_ref[at, :] = value.T.astype(BF16)
+        took(r_all.at[pl.ds(0, 3 * piece)], r_recv.at[2])
+        gathered = rows_at16(core * half_rows, half_rows)
+        remote(
+            r_all.at[gathered], r_all.at[gathered], r_send.at[3], r_recv.at[3], sibling
+        ).start()
+        took(sq_buf.at[pl.ds(0, 15)], sq_recv.at[0])
+        terms = sq_buf[0]
         for i in range(1, 16):
-            all_squares = all_squares + sq_buf[i]
+            terms = terms + sq_buf[i]
+        sq_dp[dp] = terms
+        for r in range(4):
+            for c in range(2):
+                if r or c:
+                    remote(
+                        sq_dp.at[dp], sq_dp.at[dp], sq_send.at[1], sq_recv.at[1],
+                        device(moved(pos, 1, r), lax.rem(core + c, 2)),
+                    ).start()
+        took(r_all.at[pl.ds(0, half_rows)], r_recv.at[3])
+        coef = F32((1.0 - DECAY) / math.sqrt(D))
+        for i in range(N_CHUNKS):
+            at = slice(i * CHUNK, (i + 1) * CHUNK)
+            low = jnp.dot(r_all[0:hid, :], left_t[:, at], preferred_element_type=F32)
+            blend[:, at] = (blend[:, at].astype(F32) - coef * low).astype(BF16)
+        took(sq_dp.at[pl.ds(0, 7)], sq_recv.at[1])
+        all_squares = sq_dp[0]
+        for i in range(1, 8):
+            all_squares = all_squares + sq_dp[i]
         scale = jnp.sqrt(all_squares[0:1, :] / (hid * 16) + EPS)
-        next_ref[...] = (mean / scale).astype(BF16)
+        next_ref[...] = (r_all[0:hid, :].astype(F32) / scale).astype(BF16)
 
         took(sq_buf.at[pl.ds(0, 15)], sq_send.at[0])
+        took(sq_dp.at[pl.ds(0, 7)], sq_send.at[1])
         took(r_y, r_send.at[1])
-        took(r_y, r_send.at[2])
-        took(r_core, r_send.at[3])
+        took(r_core, r_send.at[0])
+        took(r_all.at[pl.ds(0, 3 * piece)], r_send.at[2])
+        took(r_all.at[pl.ds(0, half_rows)], r_send.at[3])
         for p in range(3):
             sent(p)
-        left_out.wait()
-        keep.wait()
 
     return kernel
 
 
 def factors(momentum, gradient, right_factor):
     hid = momentum.shape[1]
-    r_rows = -(-hid // 64) * 64
+    r_rows = -(-hid // 128) * 128
     vmem = pl.BlockSpec(memory_space=pltpu.VMEM)
     hbm = pl.BlockSpec(memory_space=pl.ANY)
     return pl.pallas_call(
         make_kernel(hid, r_rows),
         out_shape=(
-            jax.ShapeDtypeStruct((hid, D), BF16),
-            jax.ShapeDtypeStruct((D, RANK), BF16),
-            jax.ShapeDtypeStruct((hid, RANK), BF16),
-            jax.ShapeDtypeStruct((hid, RANK), BF16),
+            pltpu.VMEM((1, hid, D), BF16),
+            pltpu.VMEM((D, RANK), BF16),
+            pltpu.VMEM((hid, RANK), BF16),
         ),
-        in_specs=[hbm, hbm, vmem],
-        out_specs=(hbm, hbm, vmem, vmem),
+        in_specs=[hbm, hbm, pl.BlockSpec(memory_space=pltpu.HBM)],
+        out_specs=(vmem, vmem, vmem),
         scratch_shapes=[
             pltpu.VMEM((hid, D), BF16),
-            pltpu.VMEM((hid, D), BF16),
+            pltpu.VMEM((hid, RANK), BF16),
             pltpu.VMEM((RANK, hid), BF16),
             pltpu.VMEM((D, RANK), F32),
             pltpu.VMEM((D, RANK), F32),
-            pltpu.VMEM((D, 2 * RANK), BF16),
-            pltpu.VMEM((2 * RANK, 8 * CHUNK), BF16),
+            pltpu.VMEM((2 * RANK, D), BF16),
+            pltpu.VMEM((RANK, D), BF16),
             pltpu.VMEM((hid, 2 * RANK), F32),
             pltpu.VMEM((2 * RANK, 2 * RANK), F32),
-            pltpu.VMEM((D, RANK), BF16),
             pltpu.VMEM((D // 2, RANK), F32),
             pltpu.VMEM((3, D // 8, RANK), F32),
             pltpu.VMEM((3, D // 32, RANK), F32),
@@ -481,58 +471,34 @@
             pltpu.VMEM((r_rows // 2, RANK), F32),
             pltpu.VMEM((r_rows // 2, RANK), F32),
             pltpu.VMEM((3, r_rows // 8, RANK), F32),
-            pltpu.VMEM((r_rows, RANK), F32),
+            pltpu.VMEM((r_rows, RANK), BF16),
             pltpu.VMEM((RANK, RANK), F32),
             pltpu.VMEM((RANK, RANK), F32),
             pltpu.VMEM((16, 8, RANK), F32),
+            pltpu.VMEM((8, 8, RANK), F32),
             pltpu.SemaphoreType.DMA((2, N_CHUNKS)),
+            pltpu.SemaphoreType.DMA((1,)),
             pltpu.SemaphoreType.DMA((3, STAGES)),
             pltpu.SemaphoreType.DMA((3, STAGES)),
-            pltpu.SemaphoreType.DMA((2,)),
             pltpu.SemaphoreType.DMA((4,)),
             pltpu.SemaphoreType.DMA((4,)),
-            pltpu.SemaphoreType.DMA((1,)),
-            pltpu.SemaphoreType.DMA((1,)),
+            pltpu.SemaphoreType.DMA((2,)),
+            pltpu.SemaphoreType.DMA((2,)),
         ],
         compiler_params=pltpu.CompilerParams(
-            collective_id=0, has_side_effects=True, vmem_limit_bytes=60 << 20
+            collective_id=0, has_side_effects=True, vmem_limit_bytes=40 << 20
         ),
         name="factors",
     )(momentum, gradient, right_factor)
 
 
-def feedback_kernel(blend_ref, left_ref, round_ref, out_ref):
-    low = lax.dot_general(
-        round_ref[...], left_ref[...], (((1,), (1,)), ((), ())), preferred_element_type=F32
+def shards(momentum, gradient, right_factor):
+    momentum_next, left_factor, right_next = factors(
+        momentum.swapaxes(1, 2),
+        gradient.swapaxes(1, 2),
+        pltpu.with_memory_space_constraint(right_factor, pltpu.HBM),
     )
-    coef = F32((1.0 - DECAY) / math.sqrt(D))
-    out_ref[0] = (blend_ref[...].astype(F32) - coef * low).astype(BF16)
-
-
-def feedback(blend, left_factor, right_round):
-    hid = blend.shape[0]
-    cols = 512
-    return pl.pallas_call(
-        feedback_kernel,
-        grid=(D // cols,),
-        out_shape=jax.ShapeDtypeStruct((1, hid, D), BF16),
-        in_specs=[
-            pl.BlockSpec((hid, cols), lambda i: (0, i)),
-            pl.BlockSpec((cols, RANK), lambda i: (i, 0)),
-            pl.BlockSpec((hid, RANK), lambda i: (0, 0)),
-        ],
-        out_specs=pl.BlockSpec((1, hid, cols), lambda i: (0, 0, i)),
-        compiler_params=pltpu.CompilerParams(vmem_limit_bytes=60 << 20),
-        name="feedback",
-    )(blend, left_factor, right_round)
-
-
-def shards(momentum, gradient, right_factor):
-    blend, left_factor, right_next, right_round = factors(
-        momentum.swapaxes(1, 2), gradient.swapaxes(1, 2), right_factor
-    )
-    momentum_next = feedback(blend, left_factor, right_round).swapaxes(1, 2)
-    return momentum_next, left_factor, right_next
+    return momentum_next.swapaxes(1, 2), left_factor, right_next
 
 
 def solution(mesh):

time: 82.8 us -> 70 us (0.85)
  Pallas kernels: 79.3 us -> 63.1 us
  local copies, waits for them, and re-layouts: 1.74 us -> 5.07 us
    pallas_call x2 -> x1, Pallas kernels: 79.3 us -> 63.1 us  [factors(): pl.pallas_call(make_kernel(hid, r_rows), out_shape=(pltpu.VMEM((1, hid, D...]
    unnamed x6 -> x3, local copies, waits for them, and re-layouts: 1.74 us -> 5.07 us
where the time goes in v2:
time: 70 us; the launch traced here: 68.8 us
  Pallas kernels  63.1 us (90%)
  local copies, waits for them, and re-layouts  5.07 us (7%)
    pallas_call x1, Pallas kernels, factors(): pl.pallas_call(make_kernel(hid, r_rows), out_shape=(pltpu.VMEM((1, hid, D...  63.1 us
    unnamed x3, local copies, waits for them, and re-layouts  5.07 us

profile of v2, /device:TPU:0, one launch (start us, length us, event | category | flops | bytes accessed | tf_op | source)
XLA Modules:
  0.0 68.8 jit_solution(9155533236342747159)
XLA Ops:
  0.6 63.1 %factors.1 = (bf16[1,800,5120]{2,1,0:T(8,128)(2,1)S(1)}, bf16[5120,128]{1,0:T(8,128)(2,1)S(1)}, bf16[800,128]{1,0:T(8,128)(2,1)S(1)}) custom-call(bf16[1,800,5120]{2,1,0:T(8,128)(2,1)} %bitcast.4, bf16[1,800,5120]{2,1,0:T(8,128)(2,1)} %bitcast.5, bf16[800,128]{1,0:T(8,128)(2,1)} %right_hbm.1), custom_call_target="tpu_custom_call" | custom-call | tf_op jit(solution)/shard_map/factors/pallas_call | solution.py:446
  63.8 3.3 %copy.9 = bf16[1,5120,800]{1,2,0:T(8,128)(2,1)} copy(bf16[1,5120,800]{1,2,0:T(8,128)(2,1)S(1)} %bitcast.3) | data formatting | bytes 16384000
  67.1 0.7 copy.11
  67.8 1.1 %copy.10 = bf16[5120,128]{1,0:T(8,128)(2,1)} copy(bf16[5120,128]{1,0:T(8,128)(2,1)S(1)} %get-tuple-element.10) | data formatting | bytes 2621440

commit v3 on v2

--- a/solution.py
+++ b/solution.py
@@ -18,8 +18,9 @@
 NT = (((1,), (1,)), ((), ()))
 
 CHUNK = 512
+UNIT = 256
 N_CHUNKS = D // CHUNK
-PARTS = ((0, 4, (0, 1, 2)), (4, 3, (1, 2, 0)), (7, 3, (2, 0, 1)))
+PARTS = ((0, 7, (0, 1, 2)), (7, 7, (1, 2, 0)), (14, 6, (2, 0, 1)))
 STAGES = 7
 
 
@@ -177,9 +178,9 @@
             lax.fori_loop(begin, end, one, 0)
 
         def geometry(p):
-            begin, chunks, axes = PARTS[p]
-            half = chunks * CHUNK // 2
-            base = begin * CHUNK
+            begin, units, axes = PARTS[p]
+            half = units * UNIT // 2
+            base = begin * UNIT
             own = base + core * half
             quarter = half // 4
             small = quarter // 4
@@ -492,12 +493,45 @@
     )(momentum, gradient, right_factor)
 
 
+def store_kernel(momentum_ref, left_ref, next_ref, momentum_hbm, left_hbm, next_hbm, sem):
+    rows = momentum_ref.shape[1] // 5
+    copies = [
+        pltpu.make_async_copy(
+            momentum_ref.at[0, i * rows : (i + 1) * rows],
+            momentum_hbm.at[0, i * rows : (i + 1) * rows],
+            sem.at[i],
+        )
+        for i in range(5)
+    ]
+    copies.append(pltpu.make_async_copy(left_ref, left_hbm, sem.at[5]))
+    copies.append(pltpu.make_async_copy(next_ref, next_hbm, sem.at[6]))
+    for copy in copies:
+        copy.start()
+    for copy in copies:
+        copy.wait()
+
+
+def store(*outputs):
+    vmem = pl.BlockSpec(memory_space=pltpu.VMEM)
+    hbm = pl.BlockSpec(memory_space=pltpu.HBM)
+    return pl.pallas_call(
+        store_kernel,
+        out_shape=tuple(jax.ShapeDtypeStruct(x.shape, x.dtype) for x in outputs),
+        in_specs=[vmem] * 3,
+        out_specs=(hbm,) * 3,
+        scratch_shapes=[pltpu.SemaphoreType.DMA((7,))],
+        compiler_params=pltpu.CompilerParams(vmem_limit_bytes=4 << 20),
+        name="store",
+    )(*(pltpu.with_memory_space_constraint(x, pltpu.VMEM) for x in outputs))
+
+
 def shards(momentum, gradient, right_factor):
-    momentum_next, left_factor, right_next = factors(
+    outputs = factors(
         momentum.swapaxes(1, 2),
         gradient.swapaxes(1, 2),
         pltpu.with_memory_space_constraint(right_factor, pltpu.HBM),
     )
+    momentum_next, left_factor, right_next = store(*outputs)
     return momentum_next.swapaxes(1, 2), left_factor, right_next
 
 

time: 70 us -> 67.9 us (0.970)
  local copies, waits for them, and re-layouts: 5.07 us -> 0 us
  Pallas kernels: 63.1 us -> 66.1 us
    unnamed x3 -> x0, local copies, waits for them, and re-layouts: 5.07 us -> none
    pallas_call x0 -> x1, Pallas kernels: none -> 3.74 us  [store(): pl.pallas_call(store_kernel, out_shape=tuple((jax.ShapeDtypeStruct(x.shap...]
    pallas_call x1, Pallas kernels: 63.1 us -> 62.4 us  [factors(): pl.pallas_call(make_kernel(hid, r_rows), out_shape=(pltpu.VMEM((1, hid, D...]
where the time goes in v3:
time: 67.9 us; the launch traced here: 66.8 us
  Pallas kernels  66.1 us (97%)
    pallas_call x1, Pallas kernels, factors(): pl.pallas_call(make_kernel(hid, r_rows), out_shape=(pltpu.VMEM((1, hid, D...  62.4 us
    pallas_call x1, Pallas kernels, store(): pl.pallas_call(store_kernel, out_shape=tuple((jax.ShapeDtypeStruct(x.shap...  3.74 us

profile of v3, /device:TPU:0, one launch (start us, length us, event | category | flops | bytes accessed | tf_op | source)
XLA Modules:
  0.0 66.8 jit_solution(6601956297385455334)
XLA Ops:
  0.6 62.4 %factors.1 = (bf16[1,800,5120]{2,1,0:T(8,128)(2,1)S(1)}, bf16[5120,128]{1,0:T(8,128)(2,1)S(1)}, bf16[800,128]{1,0:T(8,128)(2,1)S(1)}) custom-call(bf16[1,800,5120]{2,1,0:T(8,128)(2,1)} %bitcast.3, bf16[1,800,5120]{2,1,0:T(8,128)(2,1)} %bitcast.4, bf16[800,128]{1,0:T(8,128)(2,1)} %right_hbm.1), custom_call_target="tpu_custom_call" | custom-call | tf_op jit(solution)/shard_map/factors/pallas_call | solution.py:447
  63.0 3.7 %store.1 = (bf16[1,800,5120]{2,1,0:T(8,128)(2,1)}, bf16[5120,128]{1,0:T(8,128)(2,1)}, bf16[800,128]{1,0:T(8,128)(2,1)}) custom-call(bf16[1,800,5120]{2,1,0:T(8,128)(2,1)S(1)} %get-tuple-element.9.momentum_ref, bf16[5120,128]{1,0:T(8,128)(2,1)S(1)} %get-tuple-element.10.left_ref, bf16[800,128]{1,0:T(8,128)(2,1)S(1)} %get-tuple-element.11.next_ref), custom_call_target="tpu_custom_call" | custom-call | tf_op jit(solution)/shard_map/store/pallas_call | solution.py:517

commit v4 on v3

--- a/solution.py
+++ b/solution.py
@@ -371,11 +371,6 @@
         ) * F32(0.125)
         mine = rows_at16(core * half_rows + pos[1] * piece, piece)
         r_all[mine, :] = mean.astype(BF16)
-        for r in range(1, 4):
-            remote(
-                r_all.at[mine], r_all.at[mine],
-                r_send.at[2], r_recv.at[2], device(moved(pos, 1, r), core),
-            ).start()
         sq_buf[mp] = jnp.broadcast_to(jnp.sum(mean * mean, axis=0, keepdims=True), (8, RANK))
         for s in range(4):
             for r in range(4):
@@ -384,6 +379,11 @@
                         sq_buf.at[mp], sq_buf.at[mp], sq_send.at[0], sq_recv.at[0],
                         device(moved(moved(pos, 0, r), 2, s), core),
                     ).start()
+        for r in range(1, 4):
+            remote(
+                r_all.at[mine], r_all.at[mine],
+                r_send.at[2], r_recv.at[2], device(moved(pos, 1, r), core),
+            ).start()
 
         high, low = split(lower)
         weights = jnp.concatenate(

time: 67.9 us -> 68 us (level)
  no operation moved by 1% of the time
where the time goes in v4:
time: 68 us; the launch traced here: 66.7 us
  Pallas kernels  66.1 us (97%)
    pallas_call x1, Pallas kernels, factors(): pl.pallas_call(make_kernel(hid, r_rows), out_shape=(pltpu.VMEM((1, hid, D...  62.4 us
    pallas_call x1, Pallas kernels, store(): pl.pallas_call(store_kernel, out_shape=tuple((jax.ShapeDtypeStruct(x.shap...  3.74 us

profile of v4, /device:TPU:0, one launch (start us, length us, event | category | flops | bytes accessed | tf_op | source)
XLA Modules:
  0.0 66.7 jit_solution(3378825280295943240)
XLA Ops:
  0.6 62.4 %factors.1 = (bf16[1,800,5120]{2,1,0:T(8,128)(2,1)S(1)}, bf16[5120,128]{1,0:T(8,128)(2,1)S(1)}, bf16[800,128]{1,0:T(8,128)(2,1)S(1)}) custom-call(bf16[1,800,5120]{2,1,0:T(8,128)(2,1)} %bitcast.3, bf16[1,800,5120]{2,1,0:T(8,128)(2,1)} %bitcast.4, bf16[800,128]{1,0:T(8,128)(2,1)} %right_hbm.1), custom_call_target="tpu_custom_call" | custom-call | tf_op jit(solution)/shard_map/factors/pallas_call | solution.py:447
  63.0 3.7 %store.1 = (bf16[1,800,5120]{2,1,0:T(8,128)(2,1)}, bf16[5120,128]{1,0:T(8,128)(2,1)}, bf16[800,128]{1,0:T(8,128)(2,1)}) custom-call(bf16[1,800,5120]{2,1,0:T(8,128)(2,1)S(1)} %get-tuple-element.9.momentum_ref, bf16[5120,128]{1,0:T(8,128)(2,1)S(1)} %get-tuple-element.10.left_ref, bf16[800,128]{1,0:T(8,128)(2,1)S(1)} %get-tuple-element.11.next_ref), custom_call_target="tpu_custom_call" | custom-call | tf_op jit(solution)/shard_map/store/pallas_call | solution.py:517
